TPU v7x, 256 devices: a whole 4x4x8 slice. The times are simulated.
256 devices in a mesh: row: 16 (over x, z_lo), col: 16 (over z_hi, y, core).
Axes of the slice: x: 4, y: 4, z: 8 (z_hi: 2, z_lo: 4; z = z_hi * 4 + z_lo), core: 2. Of those that a mesh axis runs over, the one named last changes fastest.
Arguments:
- populations: float32 [19, 64, 256, 256], P(None, 'row', 'col'), may hold values from 0 to 0.5, as said below
- concentrations: float32 [2, 64, 256, 256], P(None, 'row', 'col'), may hold values from 0.5 to 1.5
- solid_mask: int32 [64, 256, 256], P('row', 'col'), may hold values 0 or 1
- charge_sites: int32 [64, 256, 256], P('row', 'col'), may hold values from 0 to 2
Outputs:
- next_populations: float32 [19, 64, 256, 256], P(None, 'row', 'col')
- next_concentrations: float32 [2, 64, 256, 256], P(None, 'row', 'col')
Inputs may be any that keep to these rules, and one draw needn't show every extreme that they name: `populations`: each population is its lattice weight w_i times a factor between 0.65 and 1.35.
All inputs are finite; a program needn't handle non-finite values. No bound on the sum of `solid_mask` on one device may be relied on, other than what follows from the above.
Results may differ from a plain program's by a relative error of at most 0.0001.
Values sent between devices are 32-bit elements; how exact they have to be, the bound alone decides.
A program may use at most 64 MiB of HBM per device.

v0:
```python
import functools
import math

import jax
import jax.numpy as jnp
import numpy as np
from jax import lax
from jax.experimental import pallas as pl
from jax.experimental.pallas import tpu as pltpu
from jax.sharding import PartitionSpec as P

DEBYE = 32
SCREEN = 1.0 / (DEBYE * DEBYE)
MESH = pl.DeviceIdType.MESH
HIGHEST = lax.Precision.HIGHEST
f32 = jnp.float32

VELOCITY = np.array(
    [[0, 0, 0], [1, 0, 0], [-1, 0, 0], [0, 1, 0], [0, -1, 0], [0, 0, 1], [0, 0, -1],
     [1, 1, 0], [-1, -1, 0], [1, -1, 0], [-1, 1, 0], [1, 0, 1], [-1, 0, -1], [1, 0, -1],
     [-1, 0, 1], [0, 1, 1], [0, -1, -1], [0, 1, -1], [0, -1, 1]]
)
OPPOSITE = [0, 2, 1, 4, 3, 6, 5, 8, 7, 10, 9, 12, 11, 14, 13, 16, 15, 18, 17]
WEIGHT = np.array([1.0 / 3.0] + [1.0 / 18.0] * 6 + [1.0 / 36.0] * 12)
SITE_CHARGE = 1.5
DIFFUSIVITY = (0.12, 0.08)
VALENCE = (1.0, -1.0)

MINUS_X = [2, 8, 10, 12, 14]
PLUS_X = [1, 7, 9, 11, 13]
REST = [0, 3, 4, 5, 6, 15, 16, 17, 18]
SLOT = {d: i for i, d in enumerate(MINUS_X)}
SLOT.update({d: 13 + i for i, d in enumerate(PLUS_X)})
SLOT.update({d: 18 + i for i, d in enumerate(REST)})
AUX = 5
N_AUX = 8
N_FIELD = 27
N_SEND = 13
Y_LOW = [7, 10, 3, 15, 17]
Y_HIGH = [9, 8, 4, 16, 18]


def collision_matrices():
    v = VELOCITY.astype(np.float64)
    x, y, z = v[:, 0], v[:, 1], v[:, 2]
    q = x * x + y * y + z * z
    rows = [
        np.ones(19), 19 * q - 30, (21 * q * q - 53 * q + 24) / 2,
        x, (5 * q - 9) * x, y, (5 * q - 9) * y, z, (5 * q - 9) * z,
        3 * x * x - q, (3 * q - 5) * (3 * x * x - q), y * y - z * z, (3 * q - 5) * (y * y - z * z),
        x * y, y * z, x * z, (y * y - z * z) * x, (z * z - x * x) * y, (x * x - y * y) * z,
    ]
    m = np.stack(rows)
    rates = np.array([0, 1.19, 1.4, 0, 1.2, 0, 1.2, 0, 1.2, 1.25, 1.4, 1.25, 1.4, 1.25, 1.25, 1.25, 1.98, 1.98, 1.98])
    inverse = m.T / np.sum(m * m, axis=1)[None, :]
    return (inverse * rates) @ m, (inverse * (1 - rates / 2)) @ m


K, G = collision_matrices()


def even_vector(f0=0.0, axis=(0, 0, 0), plane=(0, 0, 0)):
    out = np.zeros(19)
    out[0] = f0
    for i in range(1, 19):
        c = VELOCITY[i]
        if np.abs(c).sum() == 1:
            out[i] = axis[int(np.argmax(np.abs(c)))]
        else:
            out[i] = plane[int(np.argmin(np.abs(c)))]
    return out


def relax_coefficients():
    left = np.eye(19) - K
    r0 = left @ even_vector(f0=1.0)
    ra = left @ even_vector(axis=(0.5, 0, 0))
    rp = left @ even_vector(plane=(0.25, 0, 0))
    x_axis, y_axis, yz, xy = 1, 3, 15, 7
    even = {
        "rest": (r0[0], ra[0], rp[0]),
        "axis": (r0[x_axis], ra[y_axis], rp[y_axis], ra[x_axis] - ra[y_axis], rp[x_axis] - rp[y_axis]),
        "plane": (r0[xy], ra[xy], rp[xy], ra[yz] - ra[xy], rp[yz] - rp[xy]),
    }
    h = np.zeros(19)
    h[[7, 8]], h[[9, 10]] = 0.25, -0.25
    even["shear"] = (left @ h)[7]
    d = np.zeros(19)
    d[1], d[2] = 0.5, -0.5
    od = left @ d
    e = np.zeros(19)
    e[[7, 9]], e[[8, 10]] = 0.25, -0.25
    oe = left @ e
    odd = {"axis": (od[1], oe[1]), "plane": (od[7], oe[7], oe[11])}
    return even, odd


def force_coefficients():
    c = VELOCITY.astype(np.float64)

    def quad(t):
        return WEIGHT * (4.5 * np.einsum("ia,ab,ib->i", c, t, c) - 1.5 * np.trace(t))

    t = np.zeros((3, 3))
    t[0, 0] = 1.0
    qa, qb = K @ quad(t), G @ quad(t)
    qr = K @ WEIGHT
    s = np.zeros((3, 3))
    s[0, 1] = s[1, 0] = 1.0
    sa, sb = K @ quad(s), G @ quad(s)
    lj = K @ (WEIGHT * 3 * c[:, 0])
    lf = G @ (WEIGHT * 3 * c[:, 0])
    return {
        "rest": (qa[0], qb[0], qr[0]),
        "axis_trace": (qa[3], qb[3], qr[3]),
        "axis": (qa[1] - qa[3], qb[1] - qb[3]),
        "plane_trace": (qa[7], qb[7], qr[7]),
        "plane": (qa[15] - qa[7], qb[15] - qb[7]),
        "shear": (sa[7], sb[7]),
        "odd_axis": (lj[1], lf[1]),
        "odd_plane": (lj[7], lf[7]),
    }


EVEN, ODD = relax_coefficients()
FORCE = force_coefficients()
PLANES = {0: (15, 17, 1, 2), 1: (11, 13, 0, 2), 2: (7, 9, 0, 1)}


def fl(v):
    return np.float32(v)


def moments_of(f):
    pair = {i: f[i] + f[i + 1] for i in range(1, 19, 2)}
    diff = {i: f[i] - f[i + 1] for i in range(1, 19, 2)}
    s = [pair[1], pair[3], pair[5]]
    g = [pair[15] + pair[17], pair[11] + pair[13], pair[7] + pair[9]]
    ts, tg = s[0] + s[1] + s[2], g[0] + g[1] + g[2]
    density = f[0] + ts + tg
    first = {p: diff[PLANES[p][0]] + diff[PLANES[p][1]] for p in range(3)}
    second = {p: diff[PLANES[p][0]] - diff[PLANES[p][1]] for p in range(3)}
    d = [diff[1], diff[3], diff[5]]
    along = [(first[2], first[1]), (second[2], first[0]), (second[1], second[0])]
    momentum = [d[a] + along[a][0] + along[a][1] for a in range(3)]
    return pair, s, g, ts, tg, density, d, along, momentum


def relaxed(f, moments):
    pair, s, g, ts, tg, _, d, along, _ = moments
    e = EVEN
    out = [None] * 19
    out[0] = fl(e["rest"][0]) * f[0] + fl(e["rest"][1]) * ts + fl(e["rest"][2]) * tg
    ca = fl(e["axis"][0]) * f[0] + fl(e["axis"][1]) * ts + fl(e["axis"][2]) * tg
    cp = fl(e["plane"][0]) * f[0] + fl(e["plane"][1]) * ts + fl(e["plane"][2]) * tg
    odd_axis, odd_plane = [], []
    for a in range(3):
        u, w = along[a]
        odd_axis.append(fl(ODD["axis"][0]) * d[a] + fl(ODD["axis"][1]) * (u + w))
        b = fl(ODD["plane"][0]) * d[a]
        odd_plane.append(
            (b + fl(ODD["plane"][1]) * u + fl(ODD["plane"][2]) * w, b + fl(ODD["plane"][1]) * w + fl(ODD["plane"][2]) * u)
        )
    for a in range(3):
        even = ca + fl(e["axis"][3]) * s[a] + fl(e["axis"][4]) * g[a]
        out[1 + 2 * a] = even + odd_axis[a]
        out[2 + 2 * a] = even - odd_axis[a]
    parts = {
        2: (odd_plane[0][0], odd_plane[1][0]),
        1: (odd_plane[0][1], odd_plane[2][0]),
        0: (odd_plane[1][1], odd_plane[2][1]),
    }
    for p in range(3):
        i, j, _, _ = PLANES[p]
        even = cp + fl(e["plane"][3]) * s[p] + fl(e["plane"][4]) * g[p]
        shear = fl(e["shear"]) * (pair[i] - pair[j])
        u, w = parts[p]
        out[i], out[i + 1] = even + shear + (u + w), even + shear - (u + w)
        out[j], out[j + 1] = even - shear + (u - w), even - shear - (u - w)
    return out


def force_part(density, momentum, force, inverse, wanted):
    k = FORCE
    j = [momentum[a] + 0.5 * force[a] for a in range(3)]
    u = [j[a] * inverse for a in range(3)]
    aa = [j[a] * u[a] for a in range(3)]
    bb = [2.0 * (u[a] * force[a]) for a in range(3)]
    ta, tb = aa[0] + aa[1] + aa[2], bb[0] + bb[1] + bb[2]
    out = {}
    if 0 in wanted:
        out[0] = fl(k["rest"][0]) * ta + fl(k["rest"][1]) * tb + fl(k["rest"][2]) * density
    axis_common = fl(k["axis_trace"][0]) * ta + fl(k["axis_trace"][1]) * tb + fl(k["axis_trace"][2]) * density
    plane_common = fl(k["plane_trace"][0]) * ta + fl(k["plane_trace"][1]) * tb + fl(k["plane_trace"][2]) * density
    odd_plane = [fl(k["odd_plane"][0]) * j[a] + fl(k["odd_plane"][1]) * force[a] for a in range(3)]
    for a in range(3):
        ids = (1 + 2 * a, 2 + 2 * a)
        if not any(i in wanted for i in ids):
            continue
        even = axis_common + fl(k["axis"][0]) * aa[a] + fl(k["axis"][1]) * bb[a]
        odd = fl(k["odd_axis"][0]) * j[a] + fl(k["odd_axis"][1]) * force[a]
        if ids[0] in wanted:
            out[ids[0]] = even + odd
        if ids[1] in wanted:
            out[ids[1]] = even - odd
    for p in range(3):
        i1, i2, a, b = PLANES[p]
        if not any(i in wanted for i in (i1, i1 + 1, i2, i2 + 1)):
            continue
        even = plane_common + fl(k["plane"][0]) * aa[p] + fl(k["plane"][1]) * bb[p]
        shear = fl(k["shear"][0]) * (j[a] * u[b]) + fl(k["shear"][1]) * (u[a] * force[b] + u[b] * force[a])
        up, down = even + shear, even - shear
        total, apart = odd_plane[a] + odd_plane[b], odd_plane[a] - odd_plane[b]
        for i, v in ((i1, (up, total)), (i2, (down, apart))):
            if i in wanted:
                out[i] = v[0] + v[1]
            if i + 1 in wanted:
                out[i + 1] = v[0] - v[1]
    return out


def cas(rows, columns, length):
    angle = 2 * np.pi * (np.outer(rows, columns) % length) / length
    return (np.cos(angle) + np.sin(angle)).astype(np.float32)


def eigen(length):
    return 2.0 - 2.0 * np.cos(2 * np.pi * np.arange(length) / length)


def tables(nx, ny, nz):
    r = np.array([x * 4 + zl for zl in range(4) for x in range(4)])
    own_rows = np.concatenate([4 * r + xi for xi in range(4)])
    ext_rows = np.concatenate([4 * r + xx for xx in range(-1, 5)])
    c = np.arange(16)
    low = np.stack([16 * c - 1] * 6 + [16 * c - 2] * 2, axis=1).reshape(-1)
    high = np.stack([16 * c + 16] * 6 + [16 * c + 17] * 2, axis=1).reshape(-1)
    return {
        "hz": cas(np.arange(nz), np.arange(nz), nz),
        "hx": cas(np.arange(nx), own_rows % nx, nx),
        "hx_ext": cas(ext_rows % nx, np.arange(nx), nx),
        "hy_ext": cas(np.arange(ny), np.concatenate([np.arange(ny), low % ny, high % ny]), ny),
        "eig_xy": (eigen(nx)[:, None] + eigen(ny)[None, :] + SCREEN).astype(np.float32),
        "eig_z": np.broadcast_to(eigen(nz).astype(np.float32)[:, None], (nz, 128)).copy(),
    }


def near(d):
    return min(d, 4 - d)


STEPS = sorted(
    [(dx, dy, dk) for dx in range(4) for dy in range(4) for dk in range(2)],
    key=lambda t: -(near(t[0]) + near(t[1])) * 10 - t[2],
)


def dot(a, b, contract=((1,), (0,))):
    return lax.dot_general(a, b, (contract, ((), ())), precision=HIGHEST, preferred_element_type=f32)


def solve_kernel(
    pops_hbm, conc_hbm, solid_hbm, sites_hbm, hz_hbm, hx_hbm, hxe_hbm, hye_hbm, exy_hbm, ez_hbm,
    pot_ref, field, xr, yr,
    hz_ref, hx_ref, hxe_ref, hye_ref, exy_ref, ez_ref,
    pops, conc, solid, sites, sa, ra, rb, grid, sp, rp, ys, yin, cs, cin, sems, side_sems, in_sems,
):
    row, col = lax.axis_index("row"), lax.axis_index("col")
    x, zl = row // 4, lax.rem(row, 4)
    zh, y, k = col // 8, lax.rem(col // 2, 4), lax.rem(col, 2)
    z = zh * 4 + zl
    plane = y * 4 + x
    depth = z * 2 + k
    mode = depth * 16 + plane

    loads = [
        pltpu.make_async_copy(conc_hbm, conc, in_sems.at[0]),
        pltpu.make_async_copy(solid_hbm, solid, in_sems.at[1]),
        pltpu.make_async_copy(sites_hbm, sites, in_sems.at[2]),
        pltpu.make_async_copy(hz_hbm, hz_ref, in_sems.at[5]),
        pltpu.make_async_copy(pops_hbm, pops, in_sems.at[3]),
        pltpu.make_async_copy(exy_hbm, exy_ref, in_sems.at[6]),
        pltpu.make_async_copy(ez_hbm, ez_ref, in_sems.at[7]),
        pltpu.make_async_copy(hx_hbm, hx_ref, in_sems.at[8]),
        pltpu.make_async_copy(hxe_hbm, hxe_ref, in_sems.at[9]),
        pltpu.make_async_copy(hye_hbm, hye_ref, in_sems.at[10]),
    ]

    barrier = pltpu.get_barrier_semaphore()
    xs = [lax.rem(x + d, 4) for d in range(4)]
    yy = [lax.rem(y + d, 4) for d in range(4)]
    plane_peers = [(dx, dy) for dx in range(4) for dy in range(4) if (dx, dy) != (0, 0)]
    plane_peers.sort(key=lambda t: -(near(t[0]) + near(t[1])))
    depth_peers = [(dz, dk) for dz in (4, 3, 5, 2, 6, 1, 7, 0) for dk in (1, 0) if (dz, dk) != (0, 0)]
    row_up, row_down = lax.rem(row + 1, 16), lax.rem(row + 15, 16)
    col_up, col_down = lax.rem(col + 1, 16), lax.rem(col + 15, 16)

    def plane_id(dx, dy):
        return {"row": xs[dx] * 4 + zl, "col": zh * 8 + yy[dy] * 2 + k}

    def depth_pos(dz, dk):
        return lax.rem(z + dz, 8), (k if dk == 0 else 1 - k)

    def depth_id(dz, dk):
        zz, kk = depth_pos(dz, dk)
        return {"row": x * 4 + lax.rem(zz, 4), "col": (zz // 4) * 8 + y * 2 + kk}

    ids = [depth_id(*t) for t in depth_peers] + [plane_id(*t) for t in plane_peers]
    ids += [{"row": row_up, "col": col}, {"row": row_down, "col": col}, {"row": row, "col": col_up}, {"row": row, "col": col_down}]
    corner_ids = [{"row": r, "col": c} for c in (col_up, col_down) for r in (row_up, row_down)]
    ids += corner_ids
    for device in ids:
        pl.semaphore_signal(barrier, inc=1, device_id=device, device_id_type=MESH)
    for c in loads:
        c.start()

    for c in loads[:4]:
        c.wait()
    open_all = 1.0 - solid[...].astype(f32)
    kinds = sites[...]
    fixed = SITE_CHARGE * ((kinds == 1).astype(f32) - (kinds == 2).astype(f32))
    charge = (conc[0] - conc[1]) * open_all + fixed
    field[AUX + 4] = conc[0]
    field[AUX + 5] = conc[1]
    field[AUX + 6] = open_all
    field[AUX + 7] = charge
    flat = charge.reshape(64, 256)
    spectrum = dot(hz_ref[...], jnp.concatenate([flat, jnp.zeros((64, 256), f32)], axis=0), ((1,), (1,)))
    sa.reshape(256, 128)[...] = spectrum

    pl.semaphore_wait(barrier, len(ids))
    for t in depth_peers:
        zz, kk = depth_pos(*t)
        pltpu.make_async_remote_copy(
            sa.at[pl.ds((zz * 2 + kk) * 16, 16)], ra.at[zh, k, zl], sems.at[0], sems.at[1], device_id=depth_id(*t), device_id_type=MESH
        ).start()
    keep = pltpu.make_async_copy(sa.at[pl.ds(depth * 16, 16)], ra.at[zh, k, zl], in_sems.at[4])
    keep.start()

    def to_side(n, source, target, device):
        return pltpu.make_async_remote_copy(
            source, target, side_sems.at[2 * n], side_sems.at[2 * n + 1], device_id=device, device_id_type=MESH
        )

    up, down = {"row": row_up, "col": col}, {"row": row_down, "col": col}
    sides = [
        to_side(0, field.at[pl.ds(AUX + 4, 4), 3], xr.at[0, pl.ds(4, 4)], up),
        to_side(1, field.at[pl.ds(AUX + 4, 4), 0], xr.at[1, pl.ds(AUX + 4, 4)], down),
        to_side(2, field.at[pl.ds(AUX, 4), 3], xr.at[0, pl.ds(0, 4)], up),
        to_side(3, field.at[pl.ds(AUX, 4), 0], xr.at[1, pl.ds(AUX, 4)], down),
    ]
    for c in loads[4:]:
        c.wait()

    def before(i, carry):
        xx, part = lax.rem(3 * (i // 2), 4), pl.multiple_of(lax.rem(i, 2) * 8, 8)
        rows = pl.ds(part, 8)
        f = [pops[d, xx, rows, :] for d in range(19)]
        moments = moments_of(f)
        field[AUX, xx, rows, :] = moments[5]
        for a in range(3):
            field[AUX + 1 + a, xx, rows, :] = moments[8][a]
        wall = solid[xx, rows, :] == 1
        base = relaxed(f, moments)
        for d in range(19):
            field[SLOT[d], xx, rows, :] = jnp.where(wall, f[OPPOSITE[d]], base[d])
        return carry

    lax.fori_loop(0, 4, before, 0)
    late = [
        to_side(8, field.at[pl.ds(SLOT[1], 5), 3], xr.at[0, pl.ds(N_AUX, 5)], up),
        to_side(9, field.at[pl.ds(SLOT[2], 5), 0], xr.at[1, pl.ds(0, 5)], down),
    ]
    lax.fori_loop(4, 8, before, 0)
    line4 = lax.broadcasted_iota(jnp.int32, (4, 256), 0)
    for side, (edge, dirs) in enumerate(((15, Y_LOW), (0, Y_HIGH))):
        for n in range(N_SEND):
            slot = SLOT[dirs[n]] if n < 5 else AUX + n - 5
            value = field[slot, 3, edge : edge + 1, :]
            for xx in range(3):
                value = jnp.where(line4 == xx, field[slot, xx, edge : edge + 1, :], value)
            ys[side, n] = value
        for end, (xx, d) in enumerate(((3, dirs[0]), (0, dirs[1]))):
            for n in range(N_AUX):
                cs[2 * side + end, n : n + 1, :] = field[AUX + n, xx, edge : edge + 1, :]
            for n in range(N_AUX, 16):
                cs[2 * side + end, n : n + 1, :] = field[SLOT[d], xx, edge : edge + 1, :]
    sides += [to_side(10, ys.at[0], yin.at[0], {"row": row, "col": col_up}), to_side(11, ys.at[1], yin.at[1], {"row": row, "col": col_down})]
    sides += [to_side(4 + n, cs.at[n], cin.at[n], corner_ids[n]) for n in range(4)]
    for c in sides[4:]:
        c.start()

    keep.wait()
    blocks = sa.at[pl.ds(0, 240)]
    pltpu.make_async_copy(blocks, blocks, sems.at[1]).wait()
    for t in plane_peers:
        other = yy[t[1]] * 4 + xs[t[0]]
        pltpu.make_async_remote_copy(
            ra.at[:, :, :, other], rb.at[:, y, :, :, x], sems.at[6], sems.at[7], device_id=plane_id(*t), device_id_type=MESH
        ).start()
    keep = pltpu.make_async_copy(ra.at[:, :, :, plane], rb.at[:, y, :, :, x], in_sems.at[4])
    keep.start()

    for c in sides[:2]:
        c.start()
    for c in sides[2:4]:
        c.start()
    sides += late
    scale = 1.0 / ((exy_ref[...] + jnp.concatenate([ez_ref[pl.ds(mode, 1), :]] * 2, axis=1)) * float(64 * 256 * 256))
    keep.wait()
    pltpu.make_async_copy(blocks, blocks, sems.at[7]).wait()

    lane = lax.broadcasted_iota(jnp.int32, (16, 128), 1)
    sixteenth = lane // 16
    eighth = lane // 8
    in_eighth = lax.rem(lane, 8)
    arrived = rb.reshape(256, 128)
    for half in range(2):
        pieces = [arrived[(8 * half + j) * 16 : (8 * half + j + 1) * 16, :] for j in range(8)]
        for xi in range(4):
            acc = None
            for j in range(8):
                shift = (j - xi) * 16 % 128
                w = pltpu.roll(pieces[j], shift, 1) if shift else pieces[j]
                acc = w if acc is None else jnp.where(sixteenth == j, w, acc)
            grid[xi * 16 : (xi + 1) * 16, half * 128 : (half + 1) * 128] = acc
    g = dot(dot(hx_ref[...], grid[...]), hz_ref[...]) * scale
    out = dot(dot(hxe_ref[...], g), hye_ref[...])
    rims = []
    for base in (256, 384):
        merged = out[0:16, base : base + 128]
        for j in range(1, 8):
            r = {6: 0, 7: 5}.get(j, j)
            merged = jnp.where(in_eighth == j, out[r * 16 : (r + 1) * 16, base : base + 128], merged)
        rims.append(merged)
    send = sp.reshape(256, 128)
    for c in range(16):
        acc = None
        for xx in range(6):
            v = out[xx * 16 : (xx + 1) * 16, (c // 8) * 128 : (c // 8 + 1) * 128]
            shift = (xx - c % 8) * 16 % 128
            w = pltpu.roll(v, shift, 1) if shift else v
            acc = w if acc is None else jnp.where(sixteenth == xx, w, acc)
        for s in range(2):
            shift = (96 + 8 * s - 8 * c) % 128
            w = pltpu.roll(rims[s], shift, 1) if shift else rims[s]
            acc = jnp.where(eighth == 12 + s, w, acc)
        send[c * 16 : (c + 1) * 16, :] = acc

    ks = [k, 1 - k]

    def to_all(i, last):
        dz = 4 + (1 - 2 * lax.rem(i, 2)) * ((i + 1) // 2)
        zz = lax.rem(z + dz, 8)
        zr, zc = lax.rem(zz, 4), (zz // 4) * 8
        for dx, dy, dk in STEPS:
            if last and (dx, dy, dk) == (0, 0, 0):
                continue
            c = zc + yy[dy] * 2 + ks[dk]
            pltpu.make_async_remote_copy(
                sp.at[c * 16 + zr * 4 + xs[dx]], rp.at[mode], sems.at[12], sems.at[13],
                device_id={"row": xs[dx] * 4 + zr, "col": c}, device_id_type=MESH,
            ).start()

    def step(i, carry):
        to_all(i, False)
        return carry

    lax.fori_loop(0, 7, step, 0)
    to_all(7, True)
    keep = pltpu.make_async_copy(sp.at[col * 16 + zl * 4 + x], rp.at[mode], in_sems.at[4])
    keep.start()
    for c in late:
        c.start()
    for c in sides[4:10]:
        c.wait_recv()
    line = lax.broadcasted_iota(jnp.int32, (8, 256), 0)
    for side in range(2):
        for n in range(N_SEND):
            value = jnp.zeros((8, 256), f32)
            for xx in range(4):
                value = jnp.where(line == xx + 1, yin[side, n, xx : xx + 1, :], value)
            for end in range(2):
                if n >= 5 or n == end:
                    at = n - 5 if n >= 5 else N_AUX
                    value = jnp.where(line == 5 * end, cin[2 * side + end, at : at + 1, :], value)
            yr[side, n] = value
    keep.wait()
    most = rp.at[pl.ds(0, 255)]
    pltpu.make_async_copy(most, most, sems.at[13]).wait()
    pot_ref[...] = dot(rp.reshape(256, 128)[...], hz_ref[...], ((0,), (0,)))

    for c in sides[:4] + sides[10:]:
        c.wait_recv()
    pltpu.make_async_copy(blocks, blocks, sems.at[0]).wait()
    pltpu.make_async_copy(blocks, blocks, sems.at[6]).wait()
    pltpu.make_async_copy(most, most, sems.at[12]).wait()
    for c in sides:
        c.wait_send()


def solve(populations, concentrations, solid_mask, charge_sites):
    t = tables(64, 256, 256)
    vmem = pl.BlockSpec(memory_space=pltpu.VMEM)
    hbm = pl.BlockSpec(memory_space=pltpu.HBM)
    return pl.pallas_call(
        solve_kernel,
        out_shape=(
            jax.ShapeDtypeStruct((128, 256), f32),
            jax.ShapeDtypeStruct((N_FIELD, 4, 16, 256), f32),
            jax.ShapeDtypeStruct((2, N_SEND, 16, 256), f32),
            jax.ShapeDtypeStruct((2, N_SEND, 8, 256), f32),
        ),
        in_specs=[hbm] * 10,
        out_specs=(vmem,) * 4,
        scratch_shapes=[
            *[pltpu.VMEM(t[n].shape, f32) for n in TABLES],
            pltpu.VMEM((19, 4, 16, 256), f32),
            pltpu.VMEM((2, 4, 16, 256), f32),
            pltpu.VMEM((4, 16, 256), jnp.int32),
            pltpu.VMEM((4, 16, 256), jnp.int32),
            pltpu.VMEM((256, 1, 128), f32),
            pltpu.VMEM((2, 2, 4, 16, 1, 128), f32),
            pltpu.VMEM((2, 4, 2, 4, 4, 1, 128), f32),
            pltpu.VMEM((64, 256), f32),
            pltpu.VMEM((256, 1, 128), f32),
            pltpu.VMEM((256, 1, 128), f32),
            pltpu.VMEM((2, N_SEND, 4, 256), f32),
            pltpu.VMEM((2, N_SEND, 4, 256), f32),
            pltpu.VMEM((4, 16, 256), f32),
            pltpu.VMEM((4, 16, 256), f32),
            pltpu.SemaphoreType.DMA((14,)),
            pltpu.SemaphoreType.DMA((24,)),
            pltpu.SemaphoreType.DMA((11,)),
        ],
        compiler_params=pltpu.CompilerParams(collective_id=0, has_side_effects=True, vmem_limit_bytes=VMEM_A),
    )(
        *[
            pltpu.with_memory_space_constraint(v, pltpu.HBM)
            for v in (populations, concentrations, solid_mask, charge_sites, *[jnp.asarray(t[n]) for n in TABLES])
        ],
    )


TABLES = ("hz", "hx", "hx_ext", "hy_ext", "eig_xy", "eig_z")
VMEM_A = 32 * 2**20
VMEM_B = 24 * 2**20


def roll_z(v, shift):
    return pltpu.roll(v, shift % 256, 1)


def step_kernel(pot, field, xr, yr, out_hbm, conc_hbm, out, conc_out, sems):
    line16 = lax.broadcasted_iota(jnp.int32, (16, 256), 0)
    line8 = lax.broadcasted_iota(jnp.int32, (8, 256), 0)

    def up_y(v, beyond):
        return jnp.where(line16 == 15, beyond, pltpu.roll(v, 15, 0))

    def down_y(v, beyond):
        return jnp.where(line16 == 0, beyond, pltpu.roll(v, 1, 0))

    def forces(aux, electric):
        rho, mx, my, mz, c0, c1, opening = aux[:7]
        charge = -0.5 * ((c0 - c1) * opening)
        return rho * opening, [mx * opening, my * opening, mz * opening], [charge * e for e in electric], 1.0 / rho

    y_cells = []
    for side, dirs in enumerate((Y_LOW, Y_HIGH)):
        p = pot[96 + 8 * side : 104 + 8 * side, :]
        inner = jnp.zeros((8, 256), f32)
        for n in range(6):
            inner = jnp.where(line8 == n, pot[n * 16 + 15 * side : n * 16 + 15 * side + 1, :], inner)
        aux = [yr[side, 5 + n] for n in range(N_AUX)]
        left, right = pltpu.roll(p, 1, 0), pltpu.roll(p, 7, 0)
        front, back = roll_z(p, -1), roll_z(p, 1)
        rest = (6.0 + SCREEN) * p - aux[7] - inner - front - back
        given = jnp.where(line8 == 0, p[6:7, :], p[7:8, :])
        corner = (line8 == 0) | (line8 == 5)
        outer = jnp.where(corner, given, rest - left - right)
        left_all = jnp.where(line8 == 0, rest - right - outer, left)
        right_all = jnp.where(line8 == 5, rest - left - outer, right)
        along_y = inner - outer if side == 0 else outer - inner
        rho, m, force, inverse = forces(aux, (right_all - left_all, along_y, front - back))
        part = force_part(rho, m, force, inverse, dirs)
        moved = {d: roll_z(yr[side, n] + part[d], int(VELOCITY[d, 2])) for n, d in enumerate(dirs)}
        speed = aux[2] / aux[0]
        y_cells.append((p, moved, aux[4], aux[5], speed))

    planes = [pot[n * 16 : (n + 1) * 16, :] for n in range(6)]
    p_below = y_cells[0][0]
    p_above = y_cells[1][0]

    def aux_of(s):
        if s == -1:
            return [xr[0, n] for n in range(N_AUX)]
        if s == 4:
            return [xr[1, AUX + n] for n in range(N_AUX)]
        return [field[AUX + n, s] for n in range(N_AUX)]

    def base_of(d, s):
        if s == -1:
            return xr[0, SLOT[d] - AUX]
        if s == 4:
            return xr[1, SLOT[d]]
        return field[SLOT[d], s]

    def face(low, high, n):
        total = low[n] + high[n]
        return 0.25 * (low[2] + high[2]) * total - DIFFUSIVITY[n] * (
            (high[n] - low[n]) + (VALENCE[n] * 0.5) * total * (high[3] - low[3])
        )

    copies = []
    before = None
    for s in range(-1, 5):
        p = planes[s + 1]
        y_up, y_down = up_y(p, p_above[s + 1 : s + 2, :]), down_y(p, p_below[s + 1 : s + 2, :])
        front, back = roll_z(p, -1), roll_z(p, 1)
        aux = aux_of(s)
        if s == -1:
            right = planes[1]
            left = (6.0 + SCREEN) * p - aux[7] - right - y_up - y_down - front - back
            dirs = PLUS_X
        elif s == 4:
            left = planes[4]
            right = (6.0 + SCREEN) * p - aux[7] - left - y_up - y_down - front - back
            dirs = MINUS_X
        else:
            left, right = planes[s], planes[s + 2]
            dirs = [d for d in range(19) if 0 <= s + VELOCITY[d, 0] <= 3]
        rho, m, force, inverse = forces(aux, (right - left, y_up - y_down, front - back))
        part = force_part(rho, m, force, inverse, dirs)
        for d in dirs:
            cx, cy, cz = (int(n) for n in VELOCITY[d])
            v = base_of(d, s) + part[d]
            if cz:
                v = roll_z(v, cz)
            if cy == 1:
                v = down_y(v, y_cells[0][1][d][s + 1 : s + 2, :])
            elif cy == -1:
                v = up_y(v, y_cells[1][1][d][s + 1 : s + 2, :])
            out[d, s + cx] = v
        here_x = (aux[4], aux[5], aux[1] * inverse, p)
        if s >= 0:
            x_flux = [face(before[0], here_x, n) for n in range(2)]
            if s > 0:
                for n in range(2):
                    conc_out[n, s - 1] = before[1] * (before[2][n] - x_flux[n])
            if s < 4:
                uy, uz = aux[2] * inverse, aux[3] * inverse
                row = slice(s + 1, s + 2)
                here_y = (aux[4], aux[5], uy, p)
                below = tuple(down_y(v, y_cells[0][i][row, :]) for v, i in ((aux[4], 2), (aux[5], 3), (uy, 4))) + (y_down,)
                above = tuple(up_y(v, y_cells[1][i][row, :]) for v, i in ((aux[4], 2), (aux[5], 3), (uy, 4))) + (y_up,)
                here_z = (aux[4], aux[5], uz, p)
                ahead = tuple(roll_z(v, -1) for v in here_z[:3]) + (front,)
                rest = []
                for n in range(2):
                    z_flux = face(here_z, ahead, n)
                    change = face(here_y, above, n) - face(below, here_y, n) + (z_flux - roll_z(z_flux, 1))
                    rest.append(aux[4 + n] - change + x_flux[n])
                before = (here_x, aux[6], rest)
        else:
            before = (here_x,)
        if s >= 1:
            copies.append(pltpu.make_async_copy(out.at[:, s - 1], out_hbm.at[:, s - 1], sems.at[s - 1]))
            copies[-1].start()
    copies.append(pltpu.make_async_copy(conc_out, conc_hbm, sems.at[4]))
    copies[-1].start()
    for c in copies:
        c.wait()


def finish(pot, field, xr, yr):
    vmem = pl.BlockSpec(memory_space=pltpu.VMEM)
    hbm = pl.BlockSpec(memory_space=pl.ANY)
    return pl.pallas_call(
        step_kernel,
        out_shape=(jax.ShapeDtypeStruct((19, 4, 16, 256), f32), jax.ShapeDtypeStruct((2, 4, 16, 256), f32)),
        in_specs=[vmem] * 4,
        out_specs=(hbm, hbm),
        scratch_shapes=[
            pltpu.VMEM((19, 4, 16, 256), f32),
            pltpu.VMEM((2, 4, 16, 256), f32),
            pltpu.SemaphoreType.DMA((5,)),
        ],
        compiler_params=pltpu.CompilerParams(vmem_limit_bytes=VMEM_B),
    )(pot, field, xr, yr)


def per_device(populations, concentrations, solid_mask, charge_sites):
    return finish(*solve(populations, concentrations, solid_mask, charge_sites))


def solution(mesh):
    placed = (P(None, "row", "col", None), P(None, "row", "col", None), P("row", "col", None), P("row", "col", None))
    return jax.shard_map(
        per_device, mesh=mesh, in_specs=placed, out_specs=(P(None, "row", "col", None),) * 2, check_vma=False
    )
```

profile of v0, /device:TPU:1, one launch (start us, length us, event | category | flops | bytes accessed | tf_op | source)
XLA Modules:
  0.0 34.5 jit_solution(9778642276339311875)
XLA Ops:
  0.6 31.8 %shard_map.113 = (f32[128,256]{1,0:T(8,128)S(1)}, f32[27,4,16,256]{3,2,1,0:T(8,128)S(1)}, f32[2,13,16,256]{3,2,1,0:T(8,128)S(1)}, f32[2,13,8,256]{3,2,1,0:T(8,128)S(1)}) custom-call(f32[19,4,16,256]{3,2,1,0:T(8,128)} %pops_hbm.1, f32[2,4,16,256]{3,2,1,0:T(8,128)} %conc_hbm.1, s32[4,16,256]{2,1,0:T(8,128)} %solid_hbm.1, s32[4,16,256]{2,1,0:T(8,128)} %sites_hbm.1, ...), custom_call_target="tpu_custom_call" | custom-call | tf_op jit(solution)/shard_map/pallas_call | solution.py:506
  32.5 2.0 %shard_map.114 = (f32[19,4,16,256]{3,2,1,0:T(8,128)}, f32[2,4,16,256]{3,2,1,0:T(8,128)}) custom-call(f32[128,256]{1,0:T(8,128)S(1)} %get-tuple-element.6.pot, f32[27,4,16,256]{3,2,1,0:T(8,128)S(1)} %get-tuple-element.7.field, f32[2,13,16,256]{3,2,1,0:T(8,128)S(1)} %get-tuple-element.8.xr, f32[2,13,8,256]{3,2,1,0:T(8,128)S(1)} %get-tuple-element.9.yr), custom_call_target="tpu_custom_call" | custom-call | tf_op jit(solution)/shard_map/pallas_call | solution.py:679
where the time goes:
time: 34.6 us; the launch traced here: 34.5 us
  Pallas kernels  33.8 us (98%)
  between operations  0.64 us (2%)
    pallas_call x1, Pallas kernels, solve(): pl.pallas_call(solve_kernel, out_shape=(jax.ShapeDtypeStruct((128, 256),...  31.8 us
    pallas_call x1, Pallas kernels, finish(): pl.pallas_call(step_kernel, out_shape=(jax.ShapeDtypeStruct((19, 4, 16, 2...  1.98 us

commit v1 on v0

--- a/solution.py
+++ b/solution.py
@@ -325,16 +325,19 @@
     field[AUX + 6] = open_all
     field[AUX + 7] = charge
     flat = charge.reshape(64, 256)
-    spectrum = dot(hz_ref[...], jnp.concatenate([flat, jnp.zeros((64, 256), f32)], axis=0), ((1,), (1,)))
-    sa.reshape(256, 128)[...] = spectrum
+    halves = hz_ref[...].reshape(16, 2, 8, 256)
+    empty = jnp.zeros((64, 256), f32)
+    spectrum = dot(halves[:, 0].reshape(128, 256), jnp.concatenate([flat, empty], axis=0), ((1,), (1,)))
+    spectrum += dot(halves[:, 1].reshape(128, 256), jnp.concatenate([empty, flat], axis=0), ((1,), (1,)))
+    sa.reshape(128, 128)[...] = spectrum
 
     pl.semaphore_wait(barrier, len(ids))
     for t in depth_peers:
         zz, kk = depth_pos(*t)
         pltpu.make_async_remote_copy(
-            sa.at[pl.ds((zz * 2 + kk) * 16, 16)], ra.at[zh, k, zl], sems.at[0], sems.at[1], device_id=depth_id(*t), device_id_type=MESH
+            sa.at[pl.ds((zz * 2 + kk) * 8, 8)], ra.at[zh, k, zl], sems.at[0], sems.at[1], device_id=depth_id(*t), device_id_type=MESH
         ).start()
-    keep = pltpu.make_async_copy(sa.at[pl.ds(depth * 16, 16)], ra.at[zh, k, zl], in_sems.at[4])
+    keep = pltpu.make_async_copy(sa.at[pl.ds(depth * 8, 8)], ra.at[zh, k, zl], in_sems.at[4])
     keep.start()
 
     def to_side(n, source, target, device):
@@ -391,14 +394,14 @@
         c.start()
 
     keep.wait()
-    blocks = sa.at[pl.ds(0, 240)]
-    pltpu.make_async_copy(blocks, blocks, sems.at[1]).wait()
+    blocks, packed = sp.at[pl.ds(0, 240)], sa.at[pl.ds(0, 120)]
+    pltpu.make_async_copy(packed, packed, sems.at[1]).wait()
     for t in plane_peers:
         other = yy[t[1]] * 4 + xs[t[0]]
         pltpu.make_async_remote_copy(
-            ra.at[:, :, :, other], rb.at[:, y, :, :, x], sems.at[6], sems.at[7], device_id=plane_id(*t), device_id_type=MESH
+            ra.at[:, :, :, lax.rem(other, 8)], rb.at[:, y, :, :, x], sems.at[6], sems.at[7], device_id=plane_id(*t), device_id_type=MESH
         ).start()
-    keep = pltpu.make_async_copy(ra.at[:, :, :, plane], rb.at[:, y, :, :, x], in_sems.at[4])
+    keep = pltpu.make_async_copy(ra.at[:, :, :, lax.rem(plane, 8)], rb.at[:, y, :, :, x], in_sems.at[4])
     keep.start()
 
     for c in sides[:2]:
@@ -415,8 +418,10 @@
     eighth = lane // 8
     in_eighth = lax.rem(lane, 8)
     arrived = rb.reshape(256, 128)
+    upper = jnp.broadcast_to(plane, (16, 128)) >= 8
     for half in range(2):
         pieces = [arrived[(8 * half + j) * 16 : (8 * half + j + 1) * 16, :] for j in range(8)]
+        pieces = [jnp.where(upper, pltpu.roll(v, 64, 1), v) for v in pieces]
         for xi in range(4):
             acc = None
             for j in range(8):
@@ -492,7 +497,7 @@
 
     for c in sides[:4] + sides[10:]:
         c.wait_recv()
-    pltpu.make_async_copy(blocks, blocks, sems.at[0]).wait()
+    pltpu.make_async_copy(packed, packed, sems.at[0]).wait()
     pltpu.make_async_copy(blocks, blocks, sems.at[6]).wait()
     pltpu.make_async_copy(most, most, sems.at[12]).wait()
     for c in sides:
@@ -519,8 +524,8 @@
             pltpu.VMEM((2, 4, 16, 256), f32),
             pltpu.VMEM((4, 16, 256), jnp.int32),
             pltpu.VMEM((4, 16, 256), jnp.int32),
-            pltpu.VMEM((256, 1, 128), f32),
-            pltpu.VMEM((2, 2, 4, 16, 1, 128), f32),
+            pltpu.VMEM((128, 1, 128), f32),
+            pltpu.VMEM((2, 2, 4, 8, 1, 128), f32),
             pltpu.VMEM((2, 4, 2, 4, 4, 1, 128), f32),
             pltpu.VMEM((64, 256), f32),
             pltpu.VMEM((256, 1, 128), f32),

time: 34.6 us -> 33.7 us (0.974)
  Pallas kernels: 33.8 us -> 33 us
    pallas_call x1, Pallas kernels: 31.8 us -> 31 us  [solve(): pl.pallas_call(solve_kernel, out_shape=(jax.ShapeDtypeStruct((128, 256),...]
where the time goes in v1:
time: 33.7 us; the launch traced here: 33.6 us
  Pallas kernels  33 us (98%)
  between operations  0.64 us (2%)
    pallas_call x1, Pallas kernels, solve(): pl.pallas_call(solve_kernel, out_shape=(jax.ShapeDtypeStruct((128, 256),...  31 us
    pallas_call x1, Pallas kernels, finish(): pl.pallas_call(step_kernel, out_shape=(jax.ShapeDtypeStruct((19, 4, 16, 2...  1.98 us

profile of v1, /device:TPU:1, one launch (start us, length us, event | category | flops | bytes accessed | tf_op | source)
XLA Modules:
  0.0 33.6 jit_solution(13802996176449626679)
XLA Ops:
  0.6 31.0 %shard_map.113 = (f32[128,256]{1,0:T(8,128)S(1)}, f32[27,4,16,256]{3,2,1,0:T(8,128)S(1)}, f32[2,13,16,256]{3,2,1,0:T(8,128)S(1)}, f32[2,13,8,256]{3,2,1,0:T(8,128)S(1)}) custom-call(f32[19,4,16,256]{3,2,1,0:T(8,128)} %pops_hbm.1, f32[2,4,16,256]{3,2,1,0:T(8,128)} %conc_hbm.1, s32[4,16,256]{2,1,0:T(8,128)} %solid_hbm.1, s32[4,16,256]{2,1,0:T(8,128)} %sites_hbm.1, ...), custom_call_target="tpu_custom_call" | custom-call | tf_op jit(solution)/shard_map/pallas_call | solution.py:511
  31.7 2.0 %shard_map.114 = (f32[19,4,16,256]{3,2,1,0:T(8,128)}, f32[2,4,16,256]{3,2,1,0:T(8,128)}) custom-call(f32[128,256]{1,0:T(8,128)S(1)} %get-tuple-element.6.pot, f32[27,4,16,256]{3,2,1,0:T(8,128)S(1)} %get-tuple-element.7.field, f32[2,13,16,256]{3,2,1,0:T(8,128)S(1)} %get-tuple-element.8.xr, f32[2,13,8,256]{3,2,1,0:T(8,128)S(1)} %get-tuple-element.9.yr), custom_call_target="tpu_custom_call" | custom-call | tf_op jit(solution)/shard_map/pallas_call | solution.py:684

commit v2 on v1

--- a/solution.py
+++ b/solution.py
@@ -249,9 +249,13 @@
     return min(d, 4 - d)
 
 
+def hops(dx, dy, dz):
+    return near(dx) + near(dy) + min(dz, 8 - dz)
+
+
 STEPS = sorted(
-    [(dx, dy, dk) for dx in range(4) for dy in range(4) for dk in range(2)],
-    key=lambda t: -(near(t[0]) + near(t[1])) * 10 - t[2],
+    [(dx, dy, dz, dk) for dz in range(8) for dx in range(4) for dy in range(4) for dk in range(2)][1:],
+    key=lambda t: -hops(*t[:3]) * 10 - t[3],
 )
 
 
@@ -454,25 +458,17 @@
 
     ks = [k, 1 - k]
 
-    def to_all(i, last):
-        dz = 4 + (1 - 2 * lax.rem(i, 2)) * ((i + 1) // 2)
-        zz = lax.rem(z + dz, 8)
-        zr, zc = lax.rem(zz, 4), (zz // 4) * 8
-        for dx, dy, dk in STEPS:
-            if last and (dx, dy, dk) == (0, 0, 0):
-                continue
-            c = zc + yy[dy] * 2 + ks[dk]
-            pltpu.make_async_remote_copy(
-                sp.at[c * 16 + zr * 4 + xs[dx]], rp.at[mode], sems.at[12], sems.at[13],
-                device_id={"row": xs[dx] * 4 + zr, "col": c}, device_id_type=MESH,
-            ).start()
-
-    def step(i, carry):
-        to_all(i, False)
-        return carry
-
-    lax.fori_loop(0, 7, step, 0)
-    to_all(7, True)
+    zs = [lax.rem(z + d, 8) for d in range(8)]
+    x_row = [v * 4 for v in xs]
+    z_row = [lax.rem(v, 4) for v in zs]
+    yk_col = [[v * 2 + kk for kk in ks] for v in yy]
+    z_col = [(v // 4) * 8 for v in zs]
+    for n, (dx, dy, dz, dk) in enumerate(STEPS):
+        c = z_col[dz] + yk_col[dy][dk]
+        pltpu.make_async_remote_copy(
+            sp.at[c * 16 + z_row[dz] * 4 + xs[dx]], rp.at[mode], sems.at[12], sems.at[13],
+            device_id={"row": x_row[dx] + z_row[dz], "col": c}, device_id_type=MESH,
+        ).start()
     keep = pltpu.make_async_copy(sp.at[col * 16 + zl * 4 + x], rp.at[mode], in_sems.at[4])
     keep.start()
     for c in late:

time: 33.7 us -> 33.6 us (level)
  no operation moved by 1% of the time
where the time goes in v2:
time: 33.6 us; the launch traced here: 33.5 us
  Pallas kernels  32.9 us (98%)
  between operations  0.64 us (2%)
    pallas_call x1, Pallas kernels, solve(): pl.pallas_call(solve_kernel, out_shape=(jax.ShapeDtypeStruct((128, 256),...  30.9 us
    pallas_call x1, Pallas kernels, finish(): pl.pallas_call(step_kernel, out_shape=(jax.ShapeDtypeStruct((19, 4, 16, 2...  1.98 us

profile of v2, /device:TPU:1, one launch (start us, length us, event | category | flops | bytes accessed | tf_op | source)
XLA Modules:
  0.0 33.5 jit_solution(11812198052041703927)
XLA Ops:
  0.6 30.9 %shard_map.113 = (f32[128,256]{1,0:T(8,128)S(1)}, f32[27,4,16,256]{3,2,1,0:T(8,128)S(1)}, f32[2,13,16,256]{3,2,1,0:T(8,128)S(1)}, f32[2,13,8,256]{3,2,1,0:T(8,128)S(1)}) custom-call(f32[19,4,16,256]{3,2,1,0:T(8,128)} %pops_hbm.1, f32[2,4,16,256]{3,2,1,0:T(8,128)} %conc_hbm.1, s32[4,16,256]{2,1,0:T(8,128)} %solid_hbm.1, s32[4,16,256]{2,1,0:T(8,128)} %sites_hbm.1, ...), custom_call_target="tpu_custom_call" | custom-call | tf_op jit(solution)/shard_map/pallas_call | solution.py:507
  31.5 2.0 %shard_map.114 = (f32[19,4,16,256]{3,2,1,0:T(8,128)}, f32[2,4,16,256]{3,2,1,0:T(8,128)}) custom-call(f32[128,256]{1,0:T(8,128)S(1)} %get-tuple-element.6.pot, f32[27,4,16,256]{3,2,1,0:T(8,128)S(1)} %get-tuple-element.7.field, f32[2,13,16,256]{3,2,1,0:T(8,128)S(1)} %get-tuple-element.8.xr, f32[2,13,8,256]{3,2,1,0:T(8,128)S(1)} %get-tuple-element.9.yr), custom_call_target="tpu_custom_call" | custom-call | tf_op jit(solution)/shard_map/pallas_call | solution.py:680

commit v3 on v1

--- a/solution.py
+++ b/solution.py
@@ -471,10 +471,10 @@
         to_all(i, False)
         return carry
 
+    keep = pltpu.make_async_copy(sp.at[col * 16 + zl * 4 + x], rp.at[mode], in_sems.at[4])
+    keep.start()
     lax.fori_loop(0, 7, step, 0)
     to_all(7, True)
-    keep = pltpu.make_async_copy(sp.at[col * 16 + zl * 4 + x], rp.at[mode], in_sems.at[4])
-    keep.start()
     for c in late:
         c.start()
     for c in sides[4:10]:

time: 33.7 us -> 33.7 us (level)
  no operation moved by 1% of the time
where the time goes in v3:
time: 33.7 us; the launch traced here: 33.6 us
  Pallas kernels  33 us (98%)
  between operations  0.64 us (2%)
    pallas_call x1, Pallas kernels, solve(): pl.pallas_call(solve_kernel, out_shape=(jax.ShapeDtypeStruct((128, 256),...  31 us
    pallas_call x1, Pallas kernels, finish(): pl.pallas_call(step_kernel, out_shape=(jax.ShapeDtypeStruct((19, 4, 16, 2...  1.98 us

profile of v3, /device:TPU:1, one launch (start us, length us, event | category | flops | bytes accessed | tf_op | source)
XLA Modules:
  0.0 33.6 jit_solution(14678958086364330789)
XLA Ops:
  0.6 31.0 %shard_map.113 = (f32[128,256]{1,0:T(8,128)S(1)}, f32[27,4,16,256]{3,2,1,0:T(8,128)S(1)}, f32[2,13,16,256]{3,2,1,0:T(8,128)S(1)}, f32[2,13,8,256]{3,2,1,0:T(8,128)S(1)}) custom-call(f32[19,4,16,256]{3,2,1,0:T(8,128)} %pops_hbm.1, f32[2,4,16,256]{3,2,1,0:T(8,128)} %conc_hbm.1, s32[4,16,256]{2,1,0:T(8,128)} %solid_hbm.1, s32[4,16,256]{2,1,0:T(8,128)} %sites_hbm.1, ...), custom_call_target="tpu_custom_call" | custom-call | tf_op jit(solution)/shard_map/pallas_call | solution.py:511
  31.7 2.0 %shard_map.114 = (f32[19,4,16,256]{3,2,1,0:T(8,128)}, f32[2,4,16,256]{3,2,1,0:T(8,128)}) custom-call(f32[128,256]{1,0:T(8,128)S(1)} %get-tuple-element.6.pot, f32[27,4,16,256]{3,2,1,0:T(8,128)S(1)} %get-tuple-element.7.field, f32[2,13,16,256]{3,2,1,0:T(8,128)S(1)} %get-tuple-element.8.xr, f32[2,13,8,256]{3,2,1,0:T(8,128)S(1)} %get-tuple-element.9.yr), custom_call_target="tpu_custom_call" | custom-call | tf_op jit(solution)/shard_map/pallas_call | solution.py:684
